TPU v7x, 256 devices: a whole 4x4x8 slice. The times are simulated.
256 devices in a mesh: ctx: 16 (over y_hi, x, core), smp: 16 (over y_lo, z).
Axes of the slice: x: 4, y: 4 (y_hi: 2, y_lo: 2; y = y_hi * 2 + y_lo), z: 8, core: 2. Of those that a mesh axis runs over, the one named last changes fastest.
Arguments:
- hidden_states: bfloat16 [64, 64, 5120], P('smp'), may hold values from -6 to 6
- query_weight: bfloat16 [5120, 5120], P('smp', 'ctx'), may hold values from -0.078125 to 0.078125
- kv_weight: bfloat16 [5120, 2048], P('smp', 'ctx'), may hold values from -0.078125 to 0.078125
- out_weight: bfloat16 [5120, 5120], P('smp', 'ctx'), may hold values from -0.078125 to 0.078125
- query_bias: bfloat16 [5120], P('ctx'), may hold values from -3 to 3
- kv_bias: bfloat16 [2048], P('ctx'), may hold values from -3 to 3
- prompt_kv: bfloat16 [4096, 2, 1024], P('ctx')
- parents: int32 [64, 64], P('smp'), may hold values from 0 to 62, as said below
- prefix_len: int32 [64], P('smp'), may hold values from 1024 to 4096, as said below
Outputs:
- layer_out: float32 [64, 64, 5120], P('smp', None, 'ctx')
Inputs may be any that keep to these rules, and one draw needn't show every extreme that they name: parents[s, 0] = 0, and for n >= 1 the parent of node n is an earlier node. `prefix_len`: some sample sees the whole prompt.
All inputs are finite; a program needn't handle non-finite values.
Results may differ from a plain program's by a relative error of at most 0.009.
The roundings to bfloat16 on the way count: a program that leaves them out, or rounds other values in their place, can miss the bound.
Values may be sent and summed in bfloat16 or wider, within the bound.
A program may use at most 64 MiB of HBM per device.

v0:
```python
import jax
import jax.numpy as jnp
from jax import lax
from jax.sharding import PartitionSpec as P

HQ = 40
KVH = 8
HD = 128
NODES = 64
SMP_DEV = 4
PROMPT_DEV = 256
rope_theta = 1000000.0
neg_big = -1e30


def passed_along(block, axis, distance):
    devices = range(lax.axis_size(axis))
    route = [((i - distance) % len(devices), i) for i in devices]
    return lax.ppermute(block, axis, route)


def ancestors(parents):
    node_count = parents.shape[-1]
    node_ids = jnp.arange(node_count, dtype=jnp.int32)
    step_up = (parents[..., :, None] == node_ids[None, None, :]).astype(jnp.float32)
    step_up = step_up * (node_ids[:, None] > 0).astype(jnp.float32)[None]
    reach = step_up + jnp.eye(node_count, dtype=jnp.float32)[None]
    for squaring in range(max(node_count - 1, 1).bit_length()):
        reach = jnp.minimum(
            jnp.einsum("snm,smk->snk", reach, reach, precision=lax.Precision.HIGHEST), 1.0
        )
    return reach


def rotate(values, positions):
    midpoint = values.shape[-1] // 2
    frequency = rope_theta ** (-jnp.arange(midpoint, dtype=jnp.float32) / midpoint)
    angles = positions[:, None] * frequency[None, :]
    cosine = jnp.cos(angles)[:, None, :]
    sine_part = jnp.sin(angles)[:, None, :]
    lower_half = values[..., :midpoint]
    upper_half = values[..., midpoint:]
    return jnp.concatenate(
        [
            lower_half * cosine - upper_half * sine_part,
            upper_half * cosine + lower_half * sine_part,
        ],
        axis=-1,
    )


def empty_state(row_count, heads_here, group):
    return (
        jnp.full((row_count, heads_here, group), neg_big, jnp.float32),
        jnp.zeros((row_count, heads_here, group), jnp.float32),
        jnp.zeros((row_count, heads_here, group, HD), jnp.float32),
    )


def attend_block(state, queries, keys, values, allowed):
    running_max, running_sum, running_acc = state
    scores = jnp.einsum(
        "rkgd,pkd->rkgp", queries, keys, preferred_element_type=jnp.float32
    ) * HD ** (-0.5)
    wide_mask = allowed[:, None, None, :]
    scores = jnp.where(wide_mask, scores, neg_big)
    new_max = jnp.maximum(running_max, jnp.max(scores, axis=-1))
    weights = jnp.where(wide_mask, jnp.exp(scores - new_max[..., None]), 0.0)
    factor = jnp.exp(running_max - new_max)
    new_sum = running_sum * factor + jnp.sum(weights, axis=-1)
    product = jnp.einsum(
        "rkgp,pkd->rkgd", weights.astype(jnp.bfloat16), values, preferred_element_type=jnp.float32
    )
    return (new_max, new_sum, running_acc * factor[..., None] + product)


def split_block(block):
    heads_here = block.shape[2] // HD
    return (
        block[:, 0].reshape(block.shape[0], heads_here, HD),
        block[:, 1].reshape(block.shape[0], heads_here, HD),
    )


def visible(row_limits, anchor):
    key_pos = anchor * PROMPT_DEV + jnp.arange(PROMPT_DEV, dtype=jnp.int32)
    return key_pos[None, :] < row_limits[:, None]


def shards(
    hidden_states,
    query_weight,
    kv_weight,
    out_weight,
    query_bias,
    kv_bias,
    prompt_kv,
    parents,
    prefix_len,
):
    group = HQ // KVH
    ctx_size = lax.axis_size("ctx")
    ctx_index = lax.axis_index("ctx")
    tree_rows = SMP_DEV * NODES
    own_rows = tree_rows // ctx_size
    row_start = ctx_index * own_rows
    flat = hidden_states.reshape(tree_rows, hidden_states.shape[2])
    columns = flat
    query_part = jnp.dot(
        columns,
        lax.all_gather(query_weight, "smp", axis=0, tiled=True),
        preferred_element_type=jnp.float32,
    )
    kv_part = jnp.dot(
        columns,
        lax.all_gather(kv_weight, "smp", axis=0, tiled=True),
        preferred_element_type=jnp.float32,
    )
    query_part = (query_part + query_bias[None, :].astype(jnp.float32)).astype(jnp.bfloat16)
    kv_part = (kv_part + kv_bias[None, :].astype(jnp.float32)).astype(jnp.bfloat16)
    query_lin = lax.all_to_all(query_part, "ctx", split_axis=0, concat_axis=1, tiled=True)
    tree_kv = lax.all_gather(kv_part, "ctx", axis=1, tiled=True)
    reach = ancestors(parents)
    positions = (prefix_len.astype(jnp.float32)[:, None] + jnp.sum(reach, axis=-1) - 1.0).reshape(
        tree_rows
    )
    tree_keys = rotate(
        tree_kv[:, : KVH * HD].astype(jnp.float32).reshape(tree_rows, KVH, HD), positions
    ).astype(jnp.bfloat16)
    tree_values = tree_kv[:, KVH * HD :].reshape(tree_rows, KVH, HD)
    own_positions = lax.dynamic_slice_in_dim(positions, row_start, own_rows)
    queries = rotate(query_lin.astype(jnp.float32).reshape(own_rows, HQ, HD), own_positions).astype(
        jnp.bfloat16
    )
    queries = queries.reshape(own_rows, KVH, group, HD)
    row_ids = row_start + jnp.arange(own_rows, dtype=jnp.int32)
    key_ids = jnp.arange(tree_rows, dtype=jnp.int32)
    reach_rows = lax.dynamic_slice_in_dim(reach.reshape(tree_rows, NODES), row_start, own_rows)
    same_sample = row_ids[:, None] // NODES == key_ids[None, :] // NODES
    tree_allowed = same_sample & (jnp.tile(reach_rows, (1, SMP_DEV)) > 0.5)
    every_limit = jnp.repeat(prefix_len, NODES)
    limits = lax.dynamic_slice_in_dim(every_limit, row_start, own_rows)
    tree_state = attend_block(
        empty_state(own_rows, KVH, group), queries, tree_keys, tree_values, tree_allowed
    )
    local_keys, local_values = split_block(prompt_kv)
    state = attend_block(tree_state, queries, local_keys, local_values, visible(limits, ctx_index))

    def turn(step, carry):
        block, running = carry
        block = passed_along(block, "ctx", 1)
        anchor = (ctx_index - step) % ctx_size
        block_keys, block_values = split_block(block)
        return (
            block,
            attend_block(running, queries, block_keys, block_values, visible(limits, anchor)),
        )

    state = lax.fori_loop(1, ctx_size, turn, (prompt_kv, state))[1]
    attn = (state[2] / state[1][..., None]).astype(jnp.bfloat16).reshape(own_rows, HQ * HD)
    every_row = lax.all_gather(attn, "ctx", axis=0, tiled=True)
    columns = every_row
    result = jnp.dot(
        columns,
        lax.all_gather(out_weight, "smp", axis=0, tiled=True),
        preferred_element_type=jnp.float32,
    )
    return result.reshape(SMP_DEV, NODES, out_weight.shape[1])


def solution(mesh):
    return jax.shard_map(
        shards,
        mesh=mesh,
        in_specs=(
            P("smp", None, None),
            P("smp", "ctx"),
            P("smp", "ctx"),
            P("smp", "ctx"),
            P("ctx"),
            P("ctx"),
            P("ctx", None, None),
            P("smp", None),
            P("smp"),
        ),
        out_specs=P("smp", None, "ctx"),
        check_vma=False,
    )
```

profile of v0, /device:TPU:1, one launch (start us, length us, event | category | flops | bytes accessed | tf_op | source)
XLA Modules:
  0.0 659.3 jit_solution(6417092861920433570)
XLA Ops:
  8.0 65.1 %all-gather.6.cloned.1.call-done = bf16[5120,128]{1,0:T(8,128)(2,1)} async-done(((bf16[320,128]{1,0:T(8,128)(2,1)}), bf16[5120,128]{1,0:T(8,128)(2,1)}) %all-gather.6.cloned.1.call-update) | async-done | bytes 1310736 | tf_op jit(solution)/shard_map/all_gather | solution.py:116
  73.1 2.8 fusion.18
  81.1 3.6 copy.51
  84.8 2.2 fusion.48
  87.1 47.1 %all-gather.8.cloned.1.call-done = bf16[256,2048]{1,0:T(8,128)(2,1)} async-done(((bf16[256,128]{1,0:T(8,128)(2,1)}), bf16[256,2048]{1,0:T(8,128)(2,1)}) %all-gather.8.cloned.1.call-update) | async-done | bytes 1048592 | tf_op jit(solution)/shard_map/all_gather | solution.py:122
  134.2 1.3 slice_bitcast_fusion
  135.7 1.6 fusion.49
  137.4 64.6 %all-gather.10.cloned.1.call-done = bf16[5120,320]{1,0:T(8,128)(2,1)} async-done(((bf16[320,320]{1,0:T(8,128)(2,1)}), bf16[5120,320]{1,0:T(8,128)(2,1)}) %all-gather.10.cloned.1.call-update) | async-done | bytes 3276816 | tf_op jit(solution)/shard_map/all_gather | solution.py:111
  202.0 3.7 fusion.17
  206.5 15.8 %all-to-all-start = ((bf16[16,16,320]{2,1,0:T(8,128)(2,1)}), bf16[16,16,320]{2,1,0:T(8,128)(2,1)}, u32[]{:S(2)}, u32[]{:S(2)}) async-start(bf16[16,16,320]{2,1,0:T(8,128)(2,1)} %bitcast.10), calls=%async_computation | async-start | bytes 393216 | tf_op jit(solution)/shard_map/all_to_all | solution.py:121
  222.5 2.9 subtract_convert_fusion
  226.4 8.1 %all-to-all-done = bf16[16,16,320]{2,1,0:T(8,128)(2,1)} async-done(((bf16[16,16,320]{2,1,0:T(8,128)(2,1)}), bf16[16,16,320]{2,1,0:T(8,128)(2,1)}, u32[]{:S(2)}, u32[]{:S(2)}) %all-to-all-start) | async-done | bytes 163872 | tf_op jit(solution)/shard_map/all_to_all | solution.py:121
  240.5 341.6 %while.21 = (s32[]{:T(128)}, bf16[256,2,1024]{0,2,1:T(8,128)(2,1)}, f32[16,8,5]{0,2,1:T(8,128)S(1)}, f32[16,8,5]{0,2,1:T(8,128)S(1)}, f32[16,8,5,128]{3,0,2,1:T(...) while((s32[]{:T(128)}, bf16[256,2,1024]{0,2,1:T(8,128)(2,1)}, ...), condition=%wide.region_8.9_spmd, body=%wide.region_5.8_spmd.sunk | while | flops 85530128 | bytes 12282222 | solution.py:159
  240.5 1.6 collective-permute-start
  242.2 12.0 %collective-permute-done = bf16[256,2,1024]{0,2,1:T(8,128)(2,1)} collective-permute-done((bf16[256,2,1024]{0,2,1:T(8,128)(2,1)}, bf16[256,2,1024]{0,2,1:T(8,128)(2,1)}, u32[]{:S(2)}, u32[]{:S(2)}) %collective-permute-start) | collective-permute-done | bytes 1048608 | tf_op jit(solution)/shard_map/while/body/eval_jaxpr/ppermute | solution.py:19
  256.5 2.3 copy.95
  258.8 2.5 collective-permute-start
  261.4 12.0 %collective-permute-done = bf16[256,2,1024]{0,2,1:T(8,128)(2,1)} collective-permute-done((bf16[256,2,1024]{0,2,1:T(8,128)(2,1)}, bf16[256,2,1024]{0,2,1:T(8,128)(2,1)}, u32[]{:S(2)}, u32[]{:S(2)}) %collective-permute-start) | collective-permute-done | bytes 1048608 | tf_op jit(solution)/shard_map/while/body/eval_jaxpr/ppermute | solution.py:19
  275.7 2.3 copy.95
  278.1 2.5 collective-permute-start
  280.6 22.8 %collective-permute-done = bf16[256,2,1024]{0,2,1:T(8,128)(2,1)} collective-permute-done((bf16[256,2,1024]{0,2,1:T(8,128)(2,1)}, bf16[256,2,1024]{0,2,1:T(8,128)(2,1)}, u32[]{:S(2)}, u32[]{:S(2)}) %collective-permute-start) | collective-permute-done | bytes 1048608 | tf_op jit(solution)/shard_map/while/body/eval_jaxpr/ppermute | solution.py:19
  305.7 2.3 copy.95
  308.2 18.1 %collective-permute-done = bf16[256,2,1024]{0,2,1:T(8,128)(2,1)} collective-permute-done((bf16[256,2,1024]{0,2,1:T(8,128)(2,1)}, bf16[256,2,1024]{0,2,1:T(8,128)(2,1)}, u32[]{:S(2)}, u32[]{:S(2)}) %collective-permute-start) | collective-permute-done | bytes 1048608 | tf_op jit(solution)/shard_map/while/body/eval_jaxpr/ppermute | solution.py:19
  328.6 2.3 copy.95
  331.0 18.1 %collective-permute-done = bf16[256,2,1024]{0,2,1:T(8,128)(2,1)} collective-permute-done((bf16[256,2,1024]{0,2,1:T(8,128)(2,1)}, bf16[256,2,1024]{0,2,1:T(8,128)(2,1)}, u32[]{:S(2)}, u32[]{:S(2)}) %collective-permute-start) | collective-permute-done | bytes 1048608 | tf_op jit(solution)/shard_map/while/body/eval_jaxpr/ppermute | solution.py:19
  351.4 2.3 copy.95
  353.8 18.1 %collective-permute-done = bf16[256,2,1024]{0,2,1:T(8,128)(2,1)} collective-permute-done((bf16[256,2,1024]{0,2,1:T(8,128)(2,1)}, bf16[256,2,1024]{0,2,1:T(8,128)(2,1)}, u32[]{:S(2)}, u32[]{:S(2)}) %collective-permute-start) | collective-permute-done | bytes 1048608 | tf_op jit(solution)/shard_map/while/body/eval_jaxpr/ppermute | solution.py:19
  374.2 2.3 copy.95
  376.7 18.1 %collective-permute-done = bf16[256,2,1024]{0,2,1:T(8,128)(2,1)} collective-permute-done((bf16[256,2,1024]{0,2,1:T(8,128)(2,1)}, bf16[256,2,1024]{0,2,1:T(8,128)(2,1)}, u32[]{:S(2)}, u32[]{:S(2)}) %collective-permute-start) | collective-permute-done | bytes 1048608 | tf_op jit(solution)/shard_map/while/body/eval_jaxpr/ppermute | solution.py:19
  397.1 2.3 copy.95
  399.5 18.1 %collective-permute-done = bf16[256,2,1024]{0,2,1:T(8,128)(2,1)} collective-permute-done((bf16[256,2,1024]{0,2,1:T(8,128)(2,1)}, bf16[256,2,1024]{0,2,1:T(8,128)(2,1)}, u32[]{:S(2)}, u32[]{:S(2)}) %collective-permute-start) | collective-permute-done | bytes 1048608 | tf_op jit(solution)/shard_map/while/body/eval_jaxpr/ppermute | solution.py:19
  419.9 2.3 copy.95
  422.3 18.1 %collective-permute-done = bf16[256,2,1024]{0,2,1:T(8,128)(2,1)} collective-permute-done((bf16[256,2,1024]{0,2,1:T(8,128)(2,1)}, bf16[256,2,1024]{0,2,1:T(8,128)(2,1)}, u32[]{:S(2)}, u32[]{:S(2)}) %collective-permute-start) | collective-permute-done | bytes 1048608 | tf_op jit(solution)/shard_map/while/body/eval_jaxpr/ppermute | solution.py:19
  442.8 2.3 copy.95
  445.2 18.1 %collective-permute-done = bf16[256,2,1024]{0,2,1:T(8,128)(2,1)} collective-permute-done((bf16[256,2,1024]{0,2,1:T(8,128)(2,1)}, bf16[256,2,1024]{0,2,1:T(8,128)(2,1)}, u32[]{:S(2)}, u32[]{:S(2)}) %collective-permute-start) | collective-permute-done | bytes 1048608 | tf_op jit(solution)/shard_map/while/body/eval_jaxpr/ppermute | solution.py:19
  465.6 2.3 copy.95
  468.0 18.1 %collective-permute-done = bf16[256,2,1024]{0,2,1:T(8,128)(2,1)} collective-permute-done((bf16[256,2,1024]{0,2,1:T(8,128)(2,1)}, bf16[256,2,1024]{0,2,1:T(8,128)(2,1)}, u32[]{:S(2)}, u32[]{:S(2)}) %collective-permute-start) | collective-permute-done | bytes 1048608 | tf_op jit(solution)/shard_map/while/body/eval_jaxpr/ppermute | solution.py:19
  488.4 2.3 copy.95
  490.9 18.1 %collective-permute-done = bf16[256,2,1024]{0,2,1:T(8,128)(2,1)} collective-permute-done((bf16[256,2,1024]{0,2,1:T(8,128)(2,1)}, bf16[256,2,1024]{0,2,1:T(8,128)(2,1)}, u32[]{:S(2)}, u32[]{:S(2)}) %collective-permute-start) | collective-permute-done | bytes 1048608 | tf_op jit(solution)/shard_map/while/body/eval_jaxpr/ppermute | solution.py:19
  511.3 2.3 copy.95
  513.7 18.1 %collective-permute-done = bf16[256,2,1024]{0,2,1:T(8,128)(2,1)} collective-permute-done((bf16[256,2,1024]{0,2,1:T(8,128)(2,1)}, bf16[256,2,1024]{0,2,1:T(8,128)(2,1)}, u32[]{:S(2)}, u32[]{:S(2)}) %collective-permute-start) | collective-permute-done | bytes 1048608 | tf_op jit(solution)/shard_map/while/body/eval_jaxpr/ppermute | solution.py:19
  534.1 2.3 copy.95
  536.5 18.1 %collective-permute-done = bf16[256,2,1024]{0,2,1:T(8,128)(2,1)} collective-permute-done((bf16[256,2,1024]{0,2,1:T(8,128)(2,1)}, bf16[256,2,1024]{0,2,1:T(8,128)(2,1)}, u32[]{:S(2)}, u32[]{:S(2)}) %collective-permute-start) | collective-permute-done | bytes 1048608 | tf_op jit(solution)/shard_map/while/body/eval_jaxpr/ppermute | solution.py:19
  557.0 2.3 copy.95
  559.4 18.1 %collective-permute-done = bf16[256,2,1024]{0,2,1:T(8,128)(2,1)} collective-permute-done((bf16[256,2,1024]{0,2,1:T(8,128)(2,1)}, bf16[256,2,1024]{0,2,1:T(8,128)(2,1)}, u32[]{:S(2)}, u32[]{:S(2)}) %collective-permute-start) | collective-permute-done | bytes 1048608 | tf_op jit(solution)/shard_map/while/body/eval_jaxpr/ppermute | solution.py:19
  579.8 2.3 copy.95
  583.3 64.3 %all-gather.12.cloned.1.call-done = bf16[256,5120]{1,0:T(8,128)(2,1)} async-done(((bf16[16,5120]{1,0:T(8,128)(2,1)}), bf16[256,5120]{1,0:T(8,128)(2,1)}) %all-gather.12.cloned.1.call-update) | async-done | bytes 2621456 | tf_op jit(solution)/shard_map/all_gather | solution.py:161
  647.6 5.2 fusion.53
  (224 shorter events, 51.6 us)
Async XLA Ops:
  6.5 66.6 %copy-start = (bf16[4,64,5120]{2,1,0:T(8,128)(2,1)S(1)}, bf16[4,64,5120]{2,1,0:T(8,128)(2,1)}, u32[]{:S(2)}) copy-start(bf16[4,64,5120]{2,1,0:T(8,128)(2,1)} %param.11) | copy-start | bytes 7864324
  6.5 70.8 %copy-start.8 = (s32[4,64]{1,0:T(4,128)S(1)}, s32[4,64]{1,0:T(4,128)}, u32[]{:S(2)}) copy-start(s32[4,64]{1,0:T(4,128)} %param.18) | copy-start | bytes 3076
  6.5 66.6 %all-gather.6.cloned.1.call-start = ((), (), s32[]{:S(2)}) async-start(), calls=%async_computation.1 | async-start | bytes 1392640 | tf_op jit(solution)/shard_map/all_gather | solution.py:116
  7.3 126.9 %all-gather.8.cloned.1.call-start = ((), (), s32[]{:S(2)}) async-start(), calls=%async_computation.2 | async-start | bytes 1114112 | tf_op jit(solution)/shard_map/all_gather | solution.py:122
  73.1 6.0 copy-start.7
  73.1 7.6 %copy-start.6 = (bf16[320]{0:T(512)(128)(2,1)S(1)}, bf16[320]{0:T(512)(128)(2,1)}, u32[]{:S(2)}) copy-start(bf16[320]{0:T(512)(128)(2,1)} %param.15) | copy-start | bytes 1924
  76.0 126.0 %all-gather.10.cloned.1.call-start = ((), (), s32[]{:S(2)}) async-start(), calls=%async_computation.3 | async-start | bytes 4177920 | tf_op jit(solution)/shard_map/all_gather | solution.py:111
  76.7 506.6 %all-gather.14.cloned.1.call-start = ((), (), s32[]{:S(2)}) async-start(), calls=%async_computation.5 | async-start | bytes 4177920 | tf_op jit(solution)/shard_map/all_gather | solution.py:165
  206.5 28.0 %all-to-all-start = ((bf16[16,16,320]{2,1,0:T(8,128)(2,1)}), bf16[16,16,320]{2,1,0:T(8,128)(2,1)}, u32[]{:S(2)}, u32[]{:S(2)}) async-start(bf16[16,16,320]{2,1,0:T(8,128)(2,1)} %bitcast.10), calls=%async_computation | async-start | bytes 393216 | tf_op jit(solution)/shard_map/all_to_all | solution.py:121
  222.3 425.3 %all-gather.12.cloned.1.call-start = ((), (), s32[]{:S(2)}) async-start(), calls=%async_computation.4 | async-start | bytes 2785280 | tf_op jit(solution)/shard_map/all_gather | solution.py:161
  226.4 11.5 %copy-start.2 = (bf16[256,1,1024]{0,2,1:T(8,128)(2,1)S(1)}, bf16[256,1,1024]{0,2,1:T(8,128)(2,1)}, u32[]{:S(2)}) copy-start(bf16[256,1,1024]{0,2,1:T(8,128)(2,1)} %get-tuple-element.250) | copy-start | bytes 1572868
  237.5 1.0 copy-start.3
  237.5 1.2 copy-start.4
  237.9 1.9 copy-start.5
  238.7 1.4 copy-start.1
  240.5 13.6 %collective-permute-start = (bf16[256,2,1024]{0,2,1:T(8,128)(2,1)}, bf16[256,2,1024]{0,2,1:T(8,128)(2,1)}, u32[]{:S(2)}, u32[]{:S(2)}) collective-permute-start(bf16[256,2,1024]{0,2,1:T(8,128)(2,1)} %get-tuple-element.347), channel_id=1, source_target_pairs={{240,0},{0,16},{16,32},{32,48},{48,64},{64,80},{80,96},{96,112},{1... | collective-permute-start | bytes 3145736 | tf_op jit(solution)/shard_map/while/body/eval_jaxpr/ppermute | solution.py:19
  258.8 14.5 %collective-permute-start = (bf16[256,2,1024]{0,2,1:T(8,128)(2,1)}, bf16[256,2,1024]{0,2,1:T(8,128)(2,1)}, u32[]{:S(2)}, u32[]{:S(2)}) collective-permute-start(bf16[256,2,1024]{0,2,1:T(8,128)(2,1)} %get-tuple-element.347), channel_id=1, source_target_pairs={{240,0},{0,16},{16,32},{32,48},{48,64},{64,80},{80,96},{96,112},{1... | collective-permute-start | bytes 3145736 | tf_op jit(solution)/shard_map/while/body/eval_jaxpr/ppermute | solution.py:19
  278.1 25.3 %collective-permute-start = (bf16[256,2,1024]{0,2,1:T(8,128)(2,1)}, bf16[256,2,1024]{0,2,1:T(8,128)(2,1)}, u32[]{:S(2)}, u32[]{:S(2)}) collective-permute-start(bf16[256,2,1024]{0,2,1:T(8,128)(2,1)} %get-tuple-element.347), channel_id=1, source_target_pairs={{240,0},{0,16},{16,32},{32,48},{48,64},{64,80},{80,96},{96,112},{1... | collective-permute-start | bytes 3145736 | tf_op jit(solution)/shard_map/while/body/eval_jaxpr/ppermute | solution.py:19
  308.1 18.2 %collective-permute-start = (bf16[256,2,1024]{0,2,1:T(8,128)(2,1)}, bf16[256,2,1024]{0,2,1:T(8,128)(2,1)}, u32[]{:S(2)}, u32[]{:S(2)}) collective-permute-start(bf16[256,2,1024]{0,2,1:T(8,128)(2,1)} %get-tuple-element.347), channel_id=1, source_target_pairs={{240,0},{0,16},{16,32},{32,48},{48,64},{64,80},{80,96},{96,112},{1... | collective-permute-start | bytes 3145736 | tf_op jit(solution)/shard_map/while/body/eval_jaxpr/ppermute | solution.py:19
  330.9 18.2 %collective-permute-start = (bf16[256,2,1024]{0,2,1:T(8,128)(2,1)}, bf16[256,2,1024]{0,2,1:T(8,128)(2,1)}, u32[]{:S(2)}, u32[]{:S(2)}) collective-permute-start(bf16[256,2,1024]{0,2,1:T(8,128)(2,1)} %get-tuple-element.347), channel_id=1, source_target_pairs={{240,0},{0,16},{16,32},{32,48},{48,64},{64,80},{80,96},{96,112},{1... | collective-permute-start | bytes 3145736 | tf_op jit(solution)/shard_map/while/body/eval_jaxpr/ppermute | solution.py:19
  353.7 18.2 %collective-permute-start = (bf16[256,2,1024]{0,2,1:T(8,128)(2,1)}, bf16[256,2,1024]{0,2,1:T(8,128)(2,1)}, u32[]{:S(2)}, u32[]{:S(2)}) collective-permute-start(bf16[256,2,1024]{0,2,1:T(8,128)(2,1)} %get-tuple-element.347), channel_id=1, source_target_pairs={{240,0},{0,16},{16,32},{32,48},{48,64},{64,80},{80,96},{96,112},{1... | collective-permute-start | bytes 3145736 | tf_op jit(solution)/shard_map/while/body/eval_jaxpr/ppermute | solution.py:19
  376.6 18.2 %collective-permute-start = (bf16[256,2,1024]{0,2,1:T(8,128)(2,1)}, bf16[256,2,1024]{0,2,1:T(8,128)(2,1)}, u32[]{:S(2)}, u32[]{:S(2)}) collective-permute-start(bf16[256,2,1024]{0,2,1:T(8,128)(2,1)} %get-tuple-element.347), channel_id=1, source_target_pairs={{240,0},{0,16},{16,32},{32,48},{48,64},{64,80},{80,96},{96,112},{1... | collective-permute-start | bytes 3145736 | tf_op jit(solution)/shard_map/while/body/eval_jaxpr/ppermute | solution.py:19
  399.4 18.2 %collective-permute-start = (bf16[256,2,1024]{0,2,1:T(8,128)(2,1)}, bf16[256,2,1024]{0,2,1:T(8,128)(2,1)}, u32[]{:S(2)}, u32[]{:S(2)}) collective-permute-start(bf16[256,2,1024]{0,2,1:T(8,128)(2,1)} %get-tuple-element.347), channel_id=1, source_target_pairs={{240,0},{0,16},{16,32},{32,48},{48,64},{64,80},{80,96},{96,112},{1... | collective-permute-start | bytes 3145736 | tf_op jit(solution)/shard_map/while/body/eval_jaxpr/ppermute | solution.py:19
  422.3 18.2 %collective-permute-start = (bf16[256,2,1024]{0,2,1:T(8,128)(2,1)}, bf16[256,2,1024]{0,2,1:T(8,128)(2,1)}, u32[]{:S(2)}, u32[]{:S(2)}) collective-permute-start(bf16[256,2,1024]{0,2,1:T(8,128)(2,1)} %get-tuple-element.347), channel_id=1, source_target_pairs={{240,0},{0,16},{16,32},{32,48},{48,64},{64,80},{80,96},{96,112},{1... | collective-permute-start | bytes 3145736 | tf_op jit(solution)/shard_map/while/body/eval_jaxpr/ppermute | solution.py:19
  445.1 18.2 %collective-permute-start = (bf16[256,2,1024]{0,2,1:T(8,128)(2,1)}, bf16[256,2,1024]{0,2,1:T(8,128)(2,1)}, u32[]{:S(2)}, u32[]{:S(2)}) collective-permute-start(bf16[256,2,1024]{0,2,1:T(8,128)(2,1)} %get-tuple-element.347), channel_id=1, source_target_pairs={{240,0},{0,16},{16,32},{32,48},{48,64},{64,80},{80,96},{96,112},{1... | collective-permute-start | bytes 3145736 | tf_op jit(solution)/shard_map/while/body/eval_jaxpr/ppermute | solution.py:19
  467.9 18.2 %collective-permute-start = (bf16[256,2,1024]{0,2,1:T(8,128)(2,1)}, bf16[256,2,1024]{0,2,1:T(8,128)(2,1)}, u32[]{:S(2)}, u32[]{:S(2)}) collective-permute-start(bf16[256,2,1024]{0,2,1:T(8,128)(2,1)} %get-tuple-element.347), channel_id=1, source_target_pairs={{240,0},{0,16},{16,32},{32,48},{48,64},{64,80},{80,96},{96,112},{1... | collective-permute-start | bytes 3145736 | tf_op jit(solution)/shard_map/while/body/eval_jaxpr/ppermute | solution.py:19
  490.8 18.2 %collective-permute-start = (bf16[256,2,1024]{0,2,1:T(8,128)(2,1)}, bf16[256,2,1024]{0,2,1:T(8,128)(2,1)}, u32[]{:S(2)}, u32[]{:S(2)}) collective-permute-start(bf16[256,2,1024]{0,2,1:T(8,128)(2,1)} %get-tuple-element.347), channel_id=1, source_target_pairs={{240,0},{0,16},{16,32},{32,48},{48,64},{64,80},{80,96},{96,112},{1... | collective-permute-start | bytes 3145736 | tf_op jit(solution)/shard_map/while/body/eval_jaxpr/ppermute | solution.py:19
  513.6 18.2 %collective-permute-start = (bf16[256,2,1024]{0,2,1:T(8,128)(2,1)}, bf16[256,2,1024]{0,2,1:T(8,128)(2,1)}, u32[]{:S(2)}, u32[]{:S(2)}) collective-permute-start(bf16[256,2,1024]{0,2,1:T(8,128)(2,1)} %get-tuple-element.347), channel_id=1, source_target_pairs={{240,0},{0,16},{16,32},{32,48},{48,64},{64,80},{80,96},{96,112},{1... | collective-permute-start | bytes 3145736 | tf_op jit(solution)/shard_map/while/body/eval_jaxpr/ppermute | solution.py:19
  536.4 18.2 %collective-permute-start = (bf16[256,2,1024]{0,2,1:T(8,128)(2,1)}, bf16[256,2,1024]{0,2,1:T(8,128)(2,1)}, u32[]{:S(2)}, u32[]{:S(2)}) collective-permute-start(bf16[256,2,1024]{0,2,1:T(8,128)(2,1)} %get-tuple-element.347), channel_id=1, source_target_pairs={{240,0},{0,16},{16,32},{32,48},{48,64},{64,80},{80,96},{96,112},{1... | collective-permute-start | bytes 3145736 | tf_op jit(solution)/shard_map/while/body/eval_jaxpr/ppermute | solution.py:19
  559.3 18.2 %collective-permute-start = (bf16[256,2,1024]{0,2,1:T(8,128)(2,1)}, bf16[256,2,1024]{0,2,1:T(8,128)(2,1)}, u32[]{:S(2)}, u32[]{:S(2)}) collective-permute-start(bf16[256,2,1024]{0,2,1:T(8,128)(2,1)} %get-tuple-element.347), channel_id=1, source_target_pairs={{240,0},{0,16},{16,32},{32,48},{48,64},{64,80},{80,96},{96,112},{1... | collective-permute-start | bytes 3145736 | tf_op jit(solution)/shard_map/while/body/eval_jaxpr/ppermute | solution.py:19
Sparse Core Ops, SparseCore 0:
  9.1 63.9 all-gather.5
  76.1 58.0 all-gather.7
  136.0 65.9 all-gather.9
  203.6 85.2 all-gather.13
  583.4 64.1 all-gather.11
where the time goes:
time: 661 us; the launch traced here: 659 us
  waiting for transfers between devices  515 us (78%)
  local copies, waits for them, and re-layouts  67.6 us (10%)
  matrix products  25.5 us (4%)
  starting transfers between devices  22.7 us (3%)
  other arithmetic  14.6 us (2%)
  between operations  13.5 us (2%)
    ppermute x15, waiting for transfers between devices, passed_along(): return lax.ppermute(block, axis, route)  264 us
    all_gather x1, waiting for transfers between devices, shards(): lax.all_gather(kv_weight, 'smp', axis=0, tiled=True)  65.1 us
    all_gather x1, waiting for transfers between devices, shards(): lax.all_gather(query_weight, 'smp', axis=0, tiled=True)  64.6 us
    all_gather x1, waiting for transfers between devices, shards(): every_row = lax.all_gather(attn, 'ctx', axis=0, tiled=True)  64.3 us
    all_gather x1, waiting for transfers between devices, shards(): tree_kv = lax.all_gather(kv_part, 'ctx', axis=1, tiled=True)  47.1 us
    while x30, local copies, waits for them, and re-layouts  35.1 us
    slice x16, local copies, waits for them, and re-layouts, split_block(): block[:, 1].reshape(block.shape[0], heads_here, HD)  21.3 us
    all_to_all x1, starting transfers between devices, shards(): lax.all_to_all(query_part, 'ctx', split_axis=0, concat_axis=1, tiled=True)  15.8 us
  transfers between devices with their start and end apart: 21, of which 20 were waited for; matrix products, arithmetic and copies ran while one was open for 15% of the time, Pallas kernels for 0%

commit v1 on v0

--- a/solution.py
+++ b/solution.py
@@ -11,6 +11,15 @@
 PROMPT_DEV = 256
 rope_theta = 1000000.0
 neg_big = -1e30
+
+
+def touch_circles(lane_axis, x_part):
+    return jnp.concatenate(
+        lax.all_to_all(
+            jnp.stack(jnp.split(x_part, lax.psum(1, lane_axis), axis=0)), lane_axis, 0, 0
+        ),
+        axis=1,
+    )
 
 
 def passed_along(block, axis, distance):
@@ -118,7 +127,7 @@
     )
     query_part = (query_part + query_bias[None, :].astype(jnp.float32)).astype(jnp.bfloat16)
     kv_part = (kv_part + kv_bias[None, :].astype(jnp.float32)).astype(jnp.bfloat16)
-    query_lin = lax.all_to_all(query_part, "ctx", split_axis=0, concat_axis=1, tiled=True)
+    query_lin = touch_circles("ctx", x_part=query_part)
     tree_kv = lax.all_gather(kv_part, "ctx", axis=1, tiled=True)
     reach = ancestors(parents)
     positions = (prefix_len.astype(jnp.float32)[:, None] + jnp.sum(reach, axis=-1) - 1.0).reshape(

time: 661 us -> 685 us (1.036)
  local copies, waits for them, and re-layouts: 67.6 us -> 106 us
  waiting for transfers between devices: 515 us -> 496 us
    another operation x2 -> x20, local copies, waits for them, and re-layouts: 0.05 us -> 22.5 us  [the longest x18 22.5 us: touch_circles(): jnp.stack(jnp.split(x_part, lax.psum(1, lane_axis), axis=0))]
    ppermute x15, waiting for transfers between devices: 264 us -> 247 us  [passed_along(): return lax.ppermute(block, axis, route)]
    unnamed x20 -> x45, local copies, waits for them, and re-layouts: 1.62 us -> 17.7 us
  transfers between devices with their start and end apart: 21 -> 21, of which waited for: 20 -> 20; matrix products, arithmetic and copies ran while one was open for 15% -> 20% of each run, Pallas kernels for 0% -> 0%
where the time goes in v1:
time: 685 us; the launch traced here: 683 us
  waiting for transfers between devices  496 us (72%)
  local copies, waits for them, and re-layouts  106 us (15%)
  starting transfers between devices  26 us (4%)
  matrix products  25.5 us (4%)
  other arithmetic  15.1 us (2%)
  between operations  13.5 us (2%)
    ppermute x15, waiting for transfers between devices, passed_along(): return lax.ppermute(block, axis, route)  247 us
    all_gather x1, waiting for transfers between devices, shards(): lax.all_gather(kv_weight, 'smp', axis=0, tiled=True)  65.1 us
    all_gather x1, waiting for transfers between devices, shards(): lax.all_gather(query_weight, 'smp', axis=0, tiled=True)  64.6 us
    all_gather x1, waiting for transfers between devices, shards(): every_row = lax.all_gather(attn, 'ctx', axis=0, tiled=True)  63.2 us
    all_gather x1, waiting for transfers between devices, shards(): tree_kv = lax.all_gather(kv_part, 'ctx', axis=1, tiled=True)  46.5 us
    while x30, local copies, waits for them, and re-layouts  35.5 us
    another operation x18, local copies, waits for them, and re-layouts, touch_circles(): jnp.stack(jnp.split(x_part, lax.psum(1, lane_axis), axis=0))  22.5 us
    slice x16, local copies, waits for them, and re-layouts, split_block(): block[:, 1].reshape(block.shape[0], heads_here, HD)  21.3 us
  transfers between devices with their start and end apart: 21, of which 20 were waited for; matrix products, arithmetic and copies ran while one was open for 20% of the time, Pallas kernels for 0%

profile of v1, /device:TPU:1, one launch (start us, length us, event | category | flops | bytes accessed | tf_op | source)
XLA Modules:
  0.0 682.6 jit_solution(5611097748885854461)
XLA Ops:
  8.0 65.1 %all-gather.6.cloned.1.call-done = bf16[5120,128]{1,0:T(8,128)(2,1)} async-done(((bf16[320,128]{1,0:T(8,128)(2,1)}), bf16[5120,128]{1,0:T(8,128)(2,1)}) %all-gather.6.cloned.1.call-update) | async-done | bytes 1310736 | tf_op jit(solution)/shard_map/all_gather | solution.py:125
  73.1 2.8 fusion.18
  81.0 3.7 copy.133
  84.7 2.2 fusion.48
  87.7 46.5 %all-gather.8.cloned.1.call-done = bf16[256,2048]{1,0:T(8,128)(2,1)} async-done(((bf16[256,128]{1,0:T(8,128)(2,1)}), bf16[256,2048]{1,0:T(8,128)(2,1)}) %all-gather.8.cloned.1.call-update) | async-done | bytes 1048592 | tf_op jit(solution)/shard_map/all_gather | solution.py:131
  135.7 1.6 fusion.49
  137.4 64.6 %all-gather.10.cloned.1.call-done = bf16[5120,320]{1,0:T(8,128)(2,1)} async-done(((bf16[320,320]{1,0:T(8,128)(2,1)}), bf16[5120,320]{1,0:T(8,128)(2,1)}) %all-gather.10.cloned.1.call-update) | async-done | bytes 3276816 | tf_op jit(solution)/shard_map/all_gather | solution.py:120
  202.0 3.7 fusion.17
  221.1 1.6 copy.118
  244.2 15.9 %all-to-all-start = ((bf16[16,16,320]{2,1,0:T(8,128)(2,1)}), bf16[16,16,320]{2,1,0:T(8,128)(2,1)}, u32[]{:S(2)}, u32[]{:S(2)}) async-start(bf16[16,16,320]{2,1,0:T(8,128)(2,1)} %constant_dynamic-update-slice_fusion), calls=%async_computation | async-start | bytes 393216 | tf_op jit(solution)/shard_map/all_to_all | solution.py:18
  260.3 2.9 subtract_convert_fusion
  264.2 7.6 %all-to-all-done = bf16[16,16,320]{2,1,0:T(8,128)(2,1)} async-done(((bf16[16,16,320]{2,1,0:T(8,128)(2,1)}), bf16[16,16,320]{2,1,0:T(8,128)(2,1)}, u32[]{:S(2)}, u32[]{:S(2)}) %all-to-all-start) | async-done | bytes 163872 | tf_op jit(solution)/shard_map/all_to_all | solution.py:18
  277.8 328.7 %while.21 = (s32[]{:T(128)}, bf16[256,2,1024]{0,2,1:T(8,128)(2,1)}, f32[16,8,5]{0,2,1:T(8,128)S(1)}, f32[16,8,5]{0,2,1:T(8,128)S(1)}, f32[16,8,5,128]{3,0,2,1:T(...) while((s32[]{:T(128)}, bf16[256,2,1024]{0,2,1:T(8,128)(2,1)}, ...), condition=%wide.region_8.9_spmd, body=%wide.region_5.8_spmd.sunk | while | flops 85530128 | bytes 12282222 | solution.py:168
  279.2 12.0 %collective-permute-done = bf16[256,2,1024]{0,2,1:T(8,128)(2,1)} collective-permute-done((bf16[256,2,1024]{0,2,1:T(8,128)(2,1)}, bf16[256,2,1024]{0,2,1:T(8,128)(2,1)}, u32[]{:S(2)}, u32[]{:S(2)}) %collective-permute-start) | collective-permute-done | bytes 1048608 | tf_op jit(solution)/shard_map/while/body/eval_jaxpr/ppermute | solution.py:28
  293.5 2.4 copy.192
  295.9 2.5 collective-permute-start
  298.4 12.0 %collective-permute-done = bf16[256,2,1024]{0,2,1:T(8,128)(2,1)} collective-permute-done((bf16[256,2,1024]{0,2,1:T(8,128)(2,1)}, bf16[256,2,1024]{0,2,1:T(8,128)(2,1)}, u32[]{:S(2)}, u32[]{:S(2)}) %collective-permute-start) | collective-permute-done | bytes 1048608 | tf_op jit(solution)/shard_map/while/body/eval_jaxpr/ppermute | solution.py:28
  312.8 2.4 copy.192
  315.1 2.5 collective-permute-start
  317.7 12.0 %collective-permute-done = bf16[256,2,1024]{0,2,1:T(8,128)(2,1)} collective-permute-done((bf16[256,2,1024]{0,2,1:T(8,128)(2,1)}, bf16[256,2,1024]{0,2,1:T(8,128)(2,1)}, u32[]{:S(2)}, u32[]{:S(2)}) %collective-permute-start) | collective-permute-done | bytes 1048608 | tf_op jit(solution)/shard_map/while/body/eval_jaxpr/ppermute | solution.py:28
  332.0 2.4 copy.192
  334.4 2.5 collective-permute-start
  336.9 13.3 %collective-permute-done = bf16[256,2,1024]{0,2,1:T(8,128)(2,1)} collective-permute-done((bf16[256,2,1024]{0,2,1:T(8,128)(2,1)}, bf16[256,2,1024]{0,2,1:T(8,128)(2,1)}, u32[]{:S(2)}, u32[]{:S(2)}) %collective-permute-start) | collective-permute-done | bytes 1048608 | tf_op jit(solution)/shard_map/while/body/eval_jaxpr/ppermute | solution.py:28
  352.6 2.4 copy.192
  356.2 16.9 %collective-permute-done = bf16[256,2,1024]{0,2,1:T(8,128)(2,1)} collective-permute-done((bf16[256,2,1024]{0,2,1:T(8,128)(2,1)}, bf16[256,2,1024]{0,2,1:T(8,128)(2,1)}, u32[]{:S(2)}, u32[]{:S(2)}) %collective-permute-start) | collective-permute-done | bytes 1048608 | tf_op jit(solution)/shard_map/while/body/eval_jaxpr/ppermute | solution.py:28
  375.5 2.4 copy.192
  377.9 18.1 %collective-permute-done = bf16[256,2,1024]{0,2,1:T(8,128)(2,1)} collective-permute-done((bf16[256,2,1024]{0,2,1:T(8,128)(2,1)}, bf16[256,2,1024]{0,2,1:T(8,128)(2,1)}, u32[]{:S(2)}, u32[]{:S(2)}) %collective-permute-start) | collective-permute-done | bytes 1048608 | tf_op jit(solution)/shard_map/while/body/eval_jaxpr/ppermute | solution.py:28
  398.3 2.4 copy.192
  400.8 18.1 %collective-permute-done = bf16[256,2,1024]{0,2,1:T(8,128)(2,1)} collective-permute-done((bf16[256,2,1024]{0,2,1:T(8,128)(2,1)}, bf16[256,2,1024]{0,2,1:T(8,128)(2,1)}, u32[]{:S(2)}, u32[]{:S(2)}) %collective-permute-start) | collective-permute-done | bytes 1048608 | tf_op jit(solution)/shard_map/while/body/eval_jaxpr/ppermute | solution.py:28
  421.2 2.4 copy.192
  423.7 18.1 %collective-permute-done = bf16[256,2,1024]{0,2,1:T(8,128)(2,1)} collective-permute-done((bf16[256,2,1024]{0,2,1:T(8,128)(2,1)}, bf16[256,2,1024]{0,2,1:T(8,128)(2,1)}, u32[]{:S(2)}, u32[]{:S(2)}) %collective-permute-start) | collective-permute-done | bytes 1048608 | tf_op jit(solution)/shard_map/while/body/eval_jaxpr/ppermute | solution.py:28
  444.1 2.4 copy.192
  446.5 18.1 %collective-permute-done = bf16[256,2,1024]{0,2,1:T(8,128)(2,1)} collective-permute-done((bf16[256,2,1024]{0,2,1:T(8,128)(2,1)}, bf16[256,2,1024]{0,2,1:T(8,128)(2,1)}, u32[]{:S(2)}, u32[]{:S(2)}) %collective-permute-start) | collective-permute-done | bytes 1048608 | tf_op jit(solution)/shard_map/while/body/eval_jaxpr/ppermute | solution.py:28
  466.9 2.4 copy.192
  469.4 18.1 %collective-permute-done = bf16[256,2,1024]{0,2,1:T(8,128)(2,1)} collective-permute-done((bf16[256,2,1024]{0,2,1:T(8,128)(2,1)}, bf16[256,2,1024]{0,2,1:T(8,128)(2,1)}, u32[]{:S(2)}, u32[]{:S(2)}) %collective-permute-start) | collective-permute-done | bytes 1048608 | tf_op jit(solution)/shard_map/while/body/eval_jaxpr/ppermute | solution.py:28
  489.8 2.4 copy.192
  492.3 18.1 %collective-permute-done = bf16[256,2,1024]{0,2,1:T(8,128)(2,1)} collective-permute-done((bf16[256,2,1024]{0,2,1:T(8,128)(2,1)}, bf16[256,2,1024]{0,2,1:T(8,128)(2,1)}, u32[]{:S(2)}, u32[]{:S(2)}) %collective-permute-start) | collective-permute-done | bytes 1048608 | tf_op jit(solution)/shard_map/while/body/eval_jaxpr/ppermute | solution.py:28
  512.7 2.4 copy.192
  515.1 18.1 %collective-permute-done = bf16[256,2,1024]{0,2,1:T(8,128)(2,1)} collective-permute-done((bf16[256,2,1024]{0,2,1:T(8,128)(2,1)}, bf16[256,2,1024]{0,2,1:T(8,128)(2,1)}, u32[]{:S(2)}, u32[]{:S(2)}) %collective-permute-start) | collective-permute-done | bytes 1048608 | tf_op jit(solution)/shard_map/while/body/eval_jaxpr/ppermute | solution.py:28
  535.5 2.4 copy.192
  538.0 18.1 %collective-permute-done = bf16[256,2,1024]{0,2,1:T(8,128)(2,1)} collective-permute-done((bf16[256,2,1024]{0,2,1:T(8,128)(2,1)}, bf16[256,2,1024]{0,2,1:T(8,128)(2,1)}, u32[]{:S(2)}, u32[]{:S(2)}) %collective-permute-start) | collective-permute-done | bytes 1048608 | tf_op jit(solution)/shard_map/while/body/eval_jaxpr/ppermute | solution.py:28
  558.4 2.4 copy.192
  560.9 18.1 %collective-permute-done = bf16[256,2,1024]{0,2,1:T(8,128)(2,1)} collective-permute-done((bf16[256,2,1024]{0,2,1:T(8,128)(2,1)}, bf16[256,2,1024]{0,2,1:T(8,128)(2,1)}, u32[]{:S(2)}, u32[]{:S(2)}) %collective-permute-start) | collective-permute-done | bytes 1048608 | tf_op jit(solution)/shard_map/while/body/eval_jaxpr/ppermute | solution.py:28
  581.3 2.4 copy.192
  583.7 18.1 %collective-permute-done = bf16[256,2,1024]{0,2,1:T(8,128)(2,1)} collective-permute-done((bf16[256,2,1024]{0,2,1:T(8,128)(2,1)}, bf16[256,2,1024]{0,2,1:T(8,128)(2,1)}, u32[]{:S(2)}, u32[]{:S(2)}) %collective-permute-start) | collective-permute-done | bytes 1048608 | tf_op jit(solution)/shard_map/while/body/eval_jaxpr/ppermute | solution.py:28
  604.1 2.4 copy.192
  607.7 63.2 %all-gather.12.cloned.1.call-done = bf16[256,5120]{1,0:T(8,128)(2,1)} async-done(((bf16[16,5120]{1,0:T(8,128)(2,1)}), bf16[256,5120]{1,0:T(8,128)(2,1)}) %all-gather.12.cloned.1.call-update) | async-done | bytes 2621456 | tf_op jit(solution)/shard_map/all_gather | solution.py:170
  670.9 5.2 fusion.53
  (266 shorter events, 92.0 us)
Async XLA Ops:
  6.5 66.6 %copy-start = (bf16[4,64,5120]{2,1,0:T(8,128)(2,1)S(1)}, bf16[4,64,5120]{2,1,0:T(8,128)(2,1)}, u32[]{:S(2)}) copy-start(bf16[4,64,5120]{2,1,0:T(8,128)(2,1)} %param.11) | copy-start | bytes 7864324
  6.5 70.8 %copy-start.11 = (bf16[320]{0:T(512)(128)(2,1)S(1)}, bf16[320]{0:T(512)(128)(2,1)}, u32[]{:S(2)}) copy-start(bf16[320]{0:T(512)(128)(2,1)} %param.15) | copy-start | bytes 1924
  6.5 70.8 %copy-start.13 = (s32[4,64]{1,0:T(4,128)S(1)}, s32[4,64]{1,0:T(4,128)}, u32[]{:S(2)}) copy-start(s32[4,64]{1,0:T(4,128)} %param.18) | copy-start | bytes 3076
  6.5 66.6 %all-gather.6.cloned.1.call-start = ((), (), s32[]{:S(2)}) async-start(), calls=%async_computation.1 | async-start | bytes 1392640 | tf_op jit(solution)/shard_map/all_gather | solution.py:125
  7.3 126.9 %all-gather.8.cloned.1.call-start = ((), (), s32[]{:S(2)}) async-start(), calls=%async_computation.2 | async-start | bytes 1114112 | tf_op jit(solution)/shard_map/all_gather | solution.py:131
  73.1 6.0 copy-start.12
  76.0 126.0 %all-gather.10.cloned.1.call-start = ((), (), s32[]{:S(2)}) async-start(), calls=%async_computation.3 | async-start | bytes 4177920 | tf_op jit(solution)/shard_map/all_gather | solution.py:120
  76.7 531.0 %all-gather.14.cloned.1.call-start = ((), (), s32[]{:S(2)}) async-start(), calls=%async_computation.5 | async-start | bytes 4177920 | tf_op jit(solution)/shard_map/all_gather | solution.py:174
  81.0 54.5 %copy-start.9 = (s32[16]{0:T(128)}, s32[16]{0:T(128)S(1)}, u32[]{:S(2)}) copy-start(s32[16]{0:T(128)S(1)} %dynamic_slice.11) | copy-start | bytes 196
  244.2 27.5 %all-to-all-start = ((bf16[16,16,320]{2,1,0:T(8,128)(2,1)}), bf16[16,16,320]{2,1,0:T(8,128)(2,1)}, u32[]{:S(2)}, u32[]{:S(2)}) async-start(bf16[16,16,320]{2,1,0:T(8,128)(2,1)} %constant_dynamic-update-slice_fusion), calls=%async_computation | async-start | bytes 393216 | tf_op jit(solution)/shard_map/all_to_all | solution.py:18
  260.1 410.8 %all-gather.12.cloned.1.call-start = ((), (), s32[]{:S(2)}) async-start(), calls=%async_computation.4 | async-start | bytes 2785280 | tf_op jit(solution)/shard_map/all_gather | solution.py:170
  260.3 14.5 %copy-start.7 = (f32[16,64]{1,0:T(8,128)S(1)}, f32[16,64]{1,0:T(8,128)}, u32[]{:S(2)}) copy-start(f32[16,64]{1,0:T(8,128)} %get-tuple-element.294) | copy-start | bytes 12292
  260.3 14.5 %copy-start.8 = (f32[16,64]{1,0:T(8,128)S(1)}, f32[16,64]{1,0:T(8,128)}, u32[]{:S(2)}) copy-start(f32[16,64]{1,0:T(8,128)} %get-tuple-element.295) | copy-start | bytes 12292
  264.2 11.1 %copy-start.2 = (bf16[256,1,1024]{0,2,1:T(8,128)(2,1)S(1)}, bf16[256,1,1024]{0,2,1:T(8,128)(2,1)}, u32[]{:S(2)}) copy-start(bf16[256,1,1024]{0,2,1:T(8,128)(2,1)} %get-tuple-element.266) | copy-start | bytes 1572868
  272.7 2.8 copy-start.6
  274.8 1.0 copy-start.3
  274.8 1.2 copy-start.4
  275.2 1.9 copy-start.5
  276.0 1.4 copy-start.1
  276.6 1.3 copy-start.10
  277.9 13.3 %collective-permute-start = (bf16[256,2,1024]{0,2,1:T(8,128)(2,1)}, bf16[256,2,1024]{0,2,1:T(8,128)(2,1)}, u32[]{:S(2)}, u32[]{:S(2)}) collective-permute-start(bf16[256,2,1024]{0,2,1:T(8,128)(2,1)} %get-tuple-element.379), channel_id=1, source_target_pairs={{240,0},{0,16},{16,32},{32,48},{48,64},{64,80},{80,96},{96,112},{1... | collective-permute-start | bytes 3145736 | tf_op jit(solution)/shard_map/while/body/eval_jaxpr/ppermute | solution.py:28
  295.9 14.5 %collective-permute-start = (bf16[256,2,1024]{0,2,1:T(8,128)(2,1)}, bf16[256,2,1024]{0,2,1:T(8,128)(2,1)}, u32[]{:S(2)}, u32[]{:S(2)}) collective-permute-start(bf16[256,2,1024]{0,2,1:T(8,128)(2,1)} %get-tuple-element.379), channel_id=1, source_target_pairs={{240,0},{0,16},{16,32},{32,48},{48,64},{64,80},{80,96},{96,112},{1... | collective-permute-start | bytes 3145736 | tf_op jit(solution)/shard_map/while/body/eval_jaxpr/ppermute | solution.py:28
  315.1 14.5 %collective-permute-start = (bf16[256,2,1024]{0,2,1:T(8,128)(2,1)}, bf16[256,2,1024]{0,2,1:T(8,128)(2,1)}, u32[]{:S(2)}, u32[]{:S(2)}) collective-permute-start(bf16[256,2,1024]{0,2,1:T(8,128)(2,1)} %get-tuple-element.379), channel_id=1, source_target_pairs={{240,0},{0,16},{16,32},{32,48},{48,64},{64,80},{80,96},{96,112},{1... | collective-permute-start | bytes 3145736 | tf_op jit(solution)/shard_map/while/body/eval_jaxpr/ppermute | solution.py:28
  334.4 15.9 %collective-permute-start = (bf16[256,2,1024]{0,2,1:T(8,128)(2,1)}, bf16[256,2,1024]{0,2,1:T(8,128)(2,1)}, u32[]{:S(2)}, u32[]{:S(2)}) collective-permute-start(bf16[256,2,1024]{0,2,1:T(8,128)(2,1)} %get-tuple-element.379), channel_id=1, source_target_pairs={{240,0},{0,16},{16,32},{32,48},{48,64},{64,80},{80,96},{96,112},{1... | collective-permute-start | bytes 3145736 | tf_op jit(solution)/shard_map/while/body/eval_jaxpr/ppermute | solution.py:28
  355.0 18.2 %collective-permute-start = (bf16[256,2,1024]{0,2,1:T(8,128)(2,1)}, bf16[256,2,1024]{0,2,1:T(8,128)(2,1)}, u32[]{:S(2)}, u32[]{:S(2)}) collective-permute-start(bf16[256,2,1024]{0,2,1:T(8,128)(2,1)} %get-tuple-element.379), channel_id=1, source_target_pairs={{240,0},{0,16},{16,32},{32,48},{48,64},{64,80},{80,96},{96,112},{1... | collective-permute-start | bytes 3145736 | tf_op jit(solution)/shard_map/while/body/eval_jaxpr/ppermute | solution.py:28
  377.8 18.2 %collective-permute-start = (bf16[256,2,1024]{0,2,1:T(8,128)(2,1)}, bf16[256,2,1024]{0,2,1:T(8,128)(2,1)}, u32[]{:S(2)}, u32[]{:S(2)}) collective-permute-start(bf16[256,2,1024]{0,2,1:T(8,128)(2,1)} %get-tuple-element.379), channel_id=1, source_target_pairs={{240,0},{0,16},{16,32},{32,48},{48,64},{64,80},{80,96},{96,112},{1... | collective-permute-start | bytes 3145736 | tf_op jit(solution)/shard_map/while/body/eval_jaxpr/ppermute | solution.py:28
  400.7 18.2 %collective-permute-start = (bf16[256,2,1024]{0,2,1:T(8,128)(2,1)}, bf16[256,2,1024]{0,2,1:T(8,128)(2,1)}, u32[]{:S(2)}, u32[]{:S(2)}) collective-permute-start(bf16[256,2,1024]{0,2,1:T(8,128)(2,1)} %get-tuple-element.379), channel_id=1, source_target_pairs={{240,0},{0,16},{16,32},{32,48},{48,64},{64,80},{80,96},{96,112},{1... | collective-permute-start | bytes 3145736 | tf_op jit(solution)/shard_map/while/body/eval_jaxpr/ppermute | solution.py:28
  423.6 18.2 %collective-permute-start = (bf16[256,2,1024]{0,2,1:T(8,128)(2,1)}, bf16[256,2,1024]{0,2,1:T(8,128)(2,1)}, u32[]{:S(2)}, u32[]{:S(2)}) collective-permute-start(bf16[256,2,1024]{0,2,1:T(8,128)(2,1)} %get-tuple-element.379), channel_id=1, source_target_pairs={{240,0},{0,16},{16,32},{32,48},{48,64},{64,80},{80,96},{96,112},{1... | collective-permute-start | bytes 3145736 | tf_op jit(solution)/shard_map/while/body/eval_jaxpr/ppermute | solution.py:28
  446.4 18.2 %collective-permute-start = (bf16[256,2,1024]{0,2,1:T(8,128)(2,1)}, bf16[256,2,1024]{0,2,1:T(8,128)(2,1)}, u32[]{:S(2)}, u32[]{:S(2)}) collective-permute-start(bf16[256,2,1024]{0,2,1:T(8,128)(2,1)} %get-tuple-element.379), channel_id=1, source_target_pairs={{240,0},{0,16},{16,32},{32,48},{48,64},{64,80},{80,96},{96,112},{1... | collective-permute-start | bytes 3145736 | tf_op jit(solution)/shard_map/while/body/eval_jaxpr/ppermute | solution.py:28
  469.3 18.2 %collective-permute-start = (bf16[256,2,1024]{0,2,1:T(8,128)(2,1)}, bf16[256,2,1024]{0,2,1:T(8,128)(2,1)}, u32[]{:S(2)}, u32[]{:S(2)}) collective-permute-start(bf16[256,2,1024]{0,2,1:T(8,128)(2,1)} %get-tuple-element.379), channel_id=1, source_target_pairs={{240,0},{0,16},{16,32},{32,48},{48,64},{64,80},{80,96},{96,112},{1... | collective-permute-start | bytes 3145736 | tf_op jit(solution)/shard_map/while/body/eval_jaxpr/ppermute | solution.py:28
  492.2 18.2 %collective-permute-start = (bf16[256,2,1024]{0,2,1:T(8,128)(2,1)}, bf16[256,2,1024]{0,2,1:T(8,128)(2,1)}, u32[]{:S(2)}, u32[]{:S(2)}) collective-permute-start(bf16[256,2,1024]{0,2,1:T(8,128)(2,1)} %get-tuple-element.379), channel_id=1, source_target_pairs={{240,0},{0,16},{16,32},{32,48},{48,64},{64,80},{80,96},{96,112},{1... | collective-permute-start | bytes 3145736 | tf_op jit(solution)/shard_map/while/body/eval_jaxpr/ppermute | solution.py:28
  515.0 18.2 %collective-permute-start = (bf16[256,2,1024]{0,2,1:T(8,128)(2,1)}, bf16[256,2,1024]{0,2,1:T(8,128)(2,1)}, u32[]{:S(2)}, u32[]{:S(2)}) collective-permute-start(bf16[256,2,1024]{0,2,1:T(8,128)(2,1)} %get-tuple-element.379), channel_id=1, source_target_pairs={{240,0},{0,16},{16,32},{32,48},{48,64},{64,80},{80,96},{96,112},{1... | collective-permute-start | bytes 3145736 | tf_op jit(solution)/shard_map/while/body/eval_jaxpr/ppermute | solution.py:28
  537.9 18.2 %collective-permute-start = (bf16[256,2,1024]{0,2,1:T(8,128)(2,1)}, bf16[256,2,1024]{0,2,1:T(8,128)(2,1)}, u32[]{:S(2)}, u32[]{:S(2)}) collective-permute-start(bf16[256,2,1024]{0,2,1:T(8,128)(2,1)} %get-tuple-element.379), channel_id=1, source_target_pairs={{240,0},{0,16},{16,32},{32,48},{48,64},{64,80},{80,96},{96,112},{1... | collective-permute-start | bytes 3145736 | tf_op jit(solution)/shard_map/while/body/eval_jaxpr/ppermute | solution.py:28
  560.8 18.2 %collective-permute-start = (bf16[256,2,1024]{0,2,1:T(8,128)(2,1)}, bf16[256,2,1024]{0,2,1:T(8,128)(2,1)}, u32[]{:S(2)}, u32[]{:S(2)}) collective-permute-start(bf16[256,2,1024]{0,2,1:T(8,128)(2,1)} %get-tuple-element.379), channel_id=1, source_target_pairs={{240,0},{0,16},{16,32},{32,48},{48,64},{64,80},{80,96},{96,112},{1... | collective-permute-start | bytes 3145736 | tf_op jit(solution)/shard_map/while/body/eval_jaxpr/ppermute | solution.py:28
  583.6 18.2 %collective-permute-start = (bf16[256,2,1024]{0,2,1:T(8,128)(2,1)}, bf16[256,2,1024]{0,2,1:T(8,128)(2,1)}, u32[]{:S(2)}, u32[]{:S(2)}) collective-permute-start(bf16[256,2,1024]{0,2,1:T(8,128)(2,1)} %get-tuple-element.379), channel_id=1, source_target_pairs={{240,0},{0,16},{16,32},{32,48},{48,64},{64,80},{80,96},{96,112},{1... | collective-permute-start | bytes 3145736 | tf_op jit(solution)/shard_map/while/body/eval_jaxpr/ppermute | solution.py:28
Sparse Core Ops, SparseCore 0:
  9.2 63.9 all-gather.5
  76.1 58.0 all-gather.7
  136.0 65.9 all-gather.9
  203.6 73.8 all-gather.13
  607.7 63.0 all-gather.11
